TPU v7x, 128 devices: a whole 4x4x4 slice. The times are simulated.
128 devices in a mesh: tp: 4 (over y_hi, core), ep: 32 (over x, y_lo, z).
Axes of the slice: x: 4, y: 4 (y_hi: 2, y_lo: 2; y = y_hi * 2 + y_lo), z: 4, core: 2. Of those that a mesh axis runs over, the one named last changes fastest.
Arguments:
- tokens: bfloat16 [1024, 7168], P(('ep', 'tp')), may hold values from -6 to 6
- routes: int32 [1024, 2], P(('ep', 'tp')), may hold values from 0 to 3, all different within a row; in each aligned block of 8 rows (0 to 7, 8 to 15, ...) at most 8 rows name the same one
- gate_weights: float32 [1024, 2], P(('ep', 'tp')), may hold values from 0.1 to 1
- dense_gate: bfloat16 [7168, 2560], P('ep', 'tp'), may hold values from -0.0625 to 0.0625
- dense_up: bfloat16 [7168, 2560], P('ep', 'tp'), may hold values from -0.0625 to 0.0625
- dense_down: bfloat16 [7168, 2560], P('ep', 'tp'), may hold values from -0.125 to 0.125
- expert_gate: bfloat16 [4, 4864, 7168], P('tp', 'ep'), may hold values from -0.0625 to 0.0625
- expert_up: bfloat16 [4, 4864, 7168], P('tp', 'ep'), may hold values from -0.0625 to 0.0625
- expert_down: bfloat16 [4, 4864, 7168], P('tp', 'ep'), may hold values from -0.078125 to 0.078125
Outputs:
- mixed: bfloat16 [1024, 7168], P(('ep', 'tp'))
Inputs may be any that keep to these rules, and one draw needn't show every extreme that they name: `routes`: the 2 experts of a token differ. Among the 8 tokens of one device (aligned blocks of rows) no expert is named more than 8 times, and in every draw some expert is named exactly 8 times in some block; every expert is named by some token.
All inputs are finite; a program needn't handle non-finite values.
Results may differ from a plain program's by a relative error of at most 0.02.
Values may be sent and summed in bfloat16 or wider, within the bound.
A program may use at most 192 MiB of HBM per device.

v0:
```python
import jax
import jax.numpy as jnp
from jax import lax
from jax.sharding import PartitionSpec as P


def add_piece(activations, weight_piece):
    return jnp.dot(activations, weight_piece, preferred_element_type=jnp.float32)


def by_rows(left, right):
    return lax.dot_general(
        left, right, (((1,), (1,)), ((), ())), preferred_element_type=jnp.float32
    )


def per_device(
    tokens,
    routes,
    gate_weights,
    dense_gate,
    dense_up,
    dense_down,
    expert_gate,
    expert_up,
    expert_down,
):
    width = tokens.shape[1]
    local_tokens = tokens.shape[0]
    tp_count = lax.axis_size("tp")
    gathered = lax.all_gather(tokens, "tp", axis=0, tiled=True)

    def add_single(weight_piece):
        return add_piece(gathered, weight_piece)

    gate_vals = add_single(lax.all_gather(dense_gate, "ep", axis=0, tiled=True))
    up_vals = add_single(lax.all_gather(dense_up, "ep", axis=0, tiled=True))
    dense_hidden = (jax.nn.silu(gate_vals) * up_vals).astype(jnp.bfloat16)
    partial_value = by_rows(dense_hidden, lax.all_gather(dense_down, "ep", axis=0, tiled=True))
    dense_out = lax.psum_scatter(
        partial_value.astype(jnp.bfloat16), "tp", scatter_dimension=0, tiled=True
    ).astype(jnp.float32)
    entries = routes.reshape(-1)
    onehot = (entries[:, None] == jnp.arange(tp_count, dtype=jnp.int32)[None, :]).astype(jnp.int32)
    ranks = jnp.sum(jnp.cumsum(onehot, axis=0) * onehot, axis=1) - 1
    targets = (entries * local_tokens + ranks).reshape(local_tokens, 2)
    slot_ids = jnp.arange(tp_count * local_tokens, dtype=jnp.int32)
    placement = jnp.any(targets[None, :, :] == slot_ids[:, None, None], axis=2).astype(jnp.bfloat16)
    outgoing = jnp.dot(placement, tokens, preferred_element_type=jnp.float32).astype(jnp.bfloat16)
    outgoing = outgoing.reshape(tp_count, local_tokens, width)
    arrived = lax.all_to_all(outgoing, "tp", split_axis=0, concat_axis=0, tiled=True)
    arrived = arrived.reshape(-1, width)
    local_gate = expert_gate[0]
    local_up = expert_up[0]
    local_down = expert_down[0]
    piece = lax.all_gather(arrived, "ep", axis=0, tiled=True)
    e_gate = by_rows(piece, local_gate)
    e_up = by_rows(piece, local_up)
    hidden_all = (jax.nn.silu(e_gate) * e_up).astype(jnp.bfloat16)
    summed = lax.psum_scatter(
        jnp.dot(hidden_all, local_down, preferred_element_type=jnp.float32).astype(jnp.bfloat16),
        "ep",
        scatter_dimension=0,
        tiled=True,
    )
    computed = summed.reshape(tp_count, local_tokens, width)
    returned = lax.all_to_all(computed, "tp", split_axis=0, concat_axis=0, tiled=True)
    returned = returned.reshape(tp_count * local_tokens, width)
    first_rows = jnp.take(returned, targets[:, 0], axis=0).astype(jnp.float32)
    second_rows = jnp.take(returned, targets[:, 1], axis=0).astype(jnp.float32)
    routed = gate_weights[:, 0:1] * first_rows + gate_weights[:, 1:2] * second_rows
    return (tokens.astype(jnp.float32) + dense_out + routed).astype(jnp.bfloat16)


def solution(mesh):
    return jax.shard_map(
        per_device,
        mesh=mesh,
        in_specs=(
            P(("ep", "tp"), None),
            P(("ep", "tp"), None),
            P(("ep", "tp"), None),
            P("ep", "tp"),
            P("ep", "tp"),
            P("ep", "tp"),
            P("tp", "ep", None),
            P("tp", "ep", None),
            P("tp", "ep", None),
        ),
        out_specs=P(("ep", "tp"), None),
        check_vma=False,
    )
```

profile of v0, /device:TPU:1, one launch (start us, length us, event | category | flops | bytes accessed | tf_op | source)
XLA Modules:
  0.0 953.2 jit_solution(4568433679559435468)
XLA Ops:
  6.5 0.0 copy-start
  6.5 0.0 all-gather.11.cloned.1.call-start
  6.5 0.9 copy.14
  7.4 0.1 eq.28
  7.5 0.1 fusion.27
  7.6 0.2 select_reduce_fusion
  7.8 0.1 sub.6
  7.9 0.1 copy.16
  8.0 0.1 fusion.28
  8.1 1.2 fusion
  9.3 14.8 %all_to_all.10 = bf16[4,8,7168]{2,1,0:T(8,128)(2,1)} all-to-all(bf16[4,8,7168]{2,1,0:T(8,128)(2,1)S(1)} %fusion), channel_id=1, replica_groups=mesh['tp'=4,'ep'=32] {'tp'}, dimensions={0} | all-to-all | bytes 917504 | tf_op jit(solution)/shard_map/all_to_all | solution.py:51
  24.1 0.0 all-gather.11.cloned.1.call-update
  24.1 0.0 all-gather.5.cloned.1.call-start
  24.2 0.7 all-gather.5.cloned.1.call-update
  24.9 0.0 all-gather.7.cloned.1.call-start
  24.9 0.7 all-gather.7.cloned.1.call-update
  25.6 0.0 all-gather.9.cloned.1.call-start
  25.6 0.5 all-gather.9.cloned.1.call-update
  26.2 0.0 reduce-scatter.5.cloned.1.call-start
  26.2 166.3 %all-gather.11.cloned.1.call-done = bf16[1024,7168]{1,0:T(8,128)(2,1)} async-done(((bf16[32,7168]{1,0:T(8,128)(2,1)}), bf16[1024,7168]{1,0:T(8,128)(2,1)}) %all-gather.11.cloned.1.call-update) | async-done | bytes 14680080 | tf_op jit(solution)/shard_map/all_gather | solution.py:56
  192.5 10.8 %fusion.4 = f32[1024,152]{0,1:T(8,128)S(1)} fusion(bf16[1024,7168]{1,0:T(8,128)(2,1)} %all-gather.11.cloned.1.call-done, bf16[1,152,7168]{2,1,0:T(8,128)(2,1)} %param.17), kind=kOutput, calls=%fused_computation.9 | convolution fusion | flops 2231369728 | bytes 17481728 | tf_op jit(solution)/shard_map/dot_general | solution.py:12
  203.3 0.0 copy-done
  203.3 22.9 %convolution_convert_fusion = bf16[1024,7168]{1,0:T(8,128)(2,1)} fusion(bf16[1,152,7168]{2,1,0:T(8,128)(2,1)S(1)} %copy-done, bf16[1024,7168]{1,0:T(8,128)(2,1)} %all-gather.11.cloned.1.call-done, bf16[1,152,7168]{2,1,0:T(8,128)(2,1)} %param.18, f32[1024,152]{0,1:T(8,128)S(1)} %fusion.4), kind=kOutput, calls=%fused_computation.2 | convolution fusion | flops 4471013376 | bytes 34340864 | tf_op jit(solution)/shard_map/dot_general | solution.py:61
  226.3 0.0 copy-start.2
  226.3 0.0 reduce-scatter.5.cloned.1.call-update
  226.3 0.0 reduce-scatter.3.cloned.1.call-start
  226.4 0.8 copy-done.2
  227.2 30.4 %all_gather.15 = bf16[32,7168]{1,0:T(8,128)(2,1)S(1)} all-gather(bf16[8,7168]{1,0:T(8,128)(2,1)S(1)} %copy-done.2), channel_id=1, replica_groups=mesh['tp'=4,'ep'=32] {'tp'}, dimensions={0}, use_global_device_ids=true | all-gather | bytes 573440 | tf_op jit(solution)/shard_map/all_gather | solution.py:31
  257.6 99.5 %all-gather.5.cloned.1.call-done = bf16[7168,640]{1,0:T(8,128)(2,1)} async-done(((bf16[224,640]{1,0:T(8,128)(2,1)}), bf16[7168,640]{1,0:T(8,128)(2,1)}) %all-gather.5.cloned.1.call-update) | async-done | bytes 9175056 | tf_op jit(solution)/shard_map/all_gather | solution.py:36
  357.1 0.0 copy-start.1
  357.1 5.3 fusion.31
  362.4 0.0 copy-start.3
  362.4 165.4 %all-gather.7.cloned.1.call-done = bf16[7168,640]{1,0:T(8,128)(2,1)} async-done(((bf16[224,640]{1,0:T(8,128)(2,1)}), bf16[7168,640]{1,0:T(8,128)(2,1)}) %all-gather.7.cloned.1.call-update) | async-done | bytes 9175056 | tf_op jit(solution)/shard_map/all_gather | solution.py:37
  527.8 170.2 %all-gather.9.cloned.1.call-done = bf16[7168,640]{1,0:T(8,128)(2,1)} async-done(((bf16[224,640]{1,0:T(8,128)(2,1)}), bf16[7168,640]{1,0:T(8,128)(2,1)}) %all-gather.9.cloned.1.call-update) | async-done | bytes 9175056 | tf_op jit(solution)/shard_map/all_gather | solution.py:39
  698.0 11.2 %convolution_convert_fusion.2 = bf16[32,7168]{1,0:T(8,128)(2,1)} fusion(bf16[7168,640]{1,0:T(8,128)(2,1)} %all-gather.9.cloned.1.call-done, bf16[32,7168]{1,0:T(8,128)(2,1)S(1)} %all_gather.15, bf16[7168,640]{1,0:T(8,128)(2,1)} %all-gather.7.cloned.1.call-done, f32[32,640]{1,0:T(8,128)S(1)} %fusion.31), kind=kOutput, calls=%fused_computation.4 | convolution fusion | flops 587554816 | bytes 19349504 | tf_op jit(solution)/shard_map/dot_general | solution.py:12
  709.2 0.0 reduce-scatter.3.cloned.1.call-update
  709.3 0.2 slice_reduce_fusion.1
  709.5 187.1 %reduce-scatter.5.cloned.1.call-done = bf16[32,7168]{1,0:T(8,128)(2,1)} async-done(((bf16[1024,7168]{1,0:T(8,128)(2,1)}), bf16[32,7168]{1,0:T(8,128)(2,1)}) %reduce-scatter.5.cloned.1.call-update) | async-done | bytes 458768 | tf_op jit(solution)/shard_map/reduce_scatter | solution.py:60
  896.5 23.8 %all-to-all-start.1 = ((bf16[4,8,7168]{2,1,0:T(8,128)(2,1)}), bf16[4,8,7168]{2,1,0:T(8,128)(2,1)S(1)}, u32[]{:S(2)}, u32[]{:S(2)}) async-start(bf16[4,8,7168]{2,1,0:T(8,128)(2,1)} %bitcast.36), calls=%async_computation.3 | async-start | bytes 917504 | tf_op jit(solution)/shard_map/all_to_all | solution.py:67
  920.4 0.0 copy-done.3
  920.4 8.7 all-to-all-done.1
  929.1 0.6 gather_fusion
  929.7 0.6 gather_fusion.1
  930.4 14.3 %reduce-scatter.3.cloned.1.call-done = bf16[8,7168]{1,0:T(8,128)(2,1)} async-done(((bf16[32,7168]{1,0:T(8,128)(2,1)}), bf16[8,7168]{1,0:T(8,128)(2,1)}) %reduce-scatter.3.cloned.1.call-update) | async-done | bytes 114704 | tf_op jit(solution)/shard_map/reduce_scatter | solution.py:40
  944.7 1.7 add_convert_fusion
  946.4 0.0 copy-done.1
  (8 shorter events, 0.1 us)
Async XLA Ops:
  6.5 196.8 %copy-start = (bf16[1,152,7168]{2,1,0:T(8,128)(2,1)S(1)}, bf16[1,152,7168]{2,1,0:T(8,128)(2,1)}, u32[]{:S(2)}) copy-start(bf16[1,152,7168]{2,1,0:T(8,128)(2,1)} %param.19) | copy-start | bytes 6537220
  6.5 186.0 %all-gather.11.cloned.1.call-start = ((), (), s32[]{:S(2)}) async-start(), calls=%async_computation.8 | async-start | bytes 15138816 | tf_op jit(solution)/shard_map/all_gather | solution.py:56
  24.1 333.0 %all-gather.5.cloned.1.call-start = ((), (), s32[]{:S(2)}) async-start(), calls=%async_computation.4 | async-start | bytes 9461760 | tf_op jit(solution)/shard_map/all_gather | solution.py:36
  24.9 502.9 %all-gather.7.cloned.1.call-start = ((), (), s32[]{:S(2)}) async-start(), calls=%async_computation.5 | async-start | bytes 9461760 | tf_op jit(solution)/shard_map/all_gather | solution.py:37
  25.6 672.4 %all-gather.9.cloned.1.call-start = ((), (), s32[]{:S(2)}) async-start(), calls=%async_computation.6 | async-start | bytes 9461760 | tf_op jit(solution)/shard_map/all_gather | solution.py:39
  26.2 870.4 %reduce-scatter.5.cloned.1.call-start = ((), (), s32[]{:S(2)}) async-start(), calls=%async_computation.9 | async-start | bytes 15138816 | tf_op jit(solution)/shard_map/reduce_scatter | solution.py:60
  226.3 0.9 copy-start.2
  226.3 718.4 %reduce-scatter.3.cloned.1.call-start = ((), (), s32[]{:S(2)}) async-start(), calls=%async_computation.7 | async-start | bytes 573440 | tf_op jit(solution)/shard_map/reduce_scatter | solution.py:40
  357.1 589.2 %copy-start.1 = (bf16[1,152,7168]{2,1,0:T(8,128)(2,1)S(1)}, bf16[1,152,7168]{2,1,0:T(8,128)(2,1)}, u32[]{:S(2)}) copy-start(bf16[1,152,7168]{2,1,0:T(8,128)(2,1)} %param.19) | copy-start | bytes 6537220
  362.4 558.0 %copy-start.3 = (f32[8,2]{0,1:T(2,128)S(1)}, f32[8,2]{0,1:T(2,128)}, u32[]{:S(2)}) copy-start(f32[8,2]{0,1:T(2,128)} %param.13) | copy-start | bytes 196
  896.5 32.6 %all-to-all-start.1 = ((bf16[4,8,7168]{2,1,0:T(8,128)(2,1)}), bf16[4,8,7168]{2,1,0:T(8,128)(2,1)S(1)}, u32[]{:S(2)}, u32[]{:S(2)}) async-start(bf16[4,8,7168]{2,1,0:T(8,128)(2,1)} %bitcast.36), calls=%async_computation.3 | async-start | bytes 917504 | tf_op jit(solution)/shard_map/all_to_all | solution.py:67
Sparse Core Ops, SparseCore 0:
  24.2 168.2 all-gather.10
  194.2 162.8 all-gather.4
  358.8 168.9 all-gather.6
  529.3 168.6 all-gather.8
  700.3 196.2 reduce-scatter.4
  899.0 45.6 reduce-scatter.2
where the time goes:
time: 954 us; the launch traced here: 953 us
  waiting for transfers between devices  814 us (85%)
  matrix products  51.4 us (5%)
  blocking collectives  45.2 us (5%)
  starting transfers between devices  24 us (3%)
  between operations  13.6 us (1%)
    reduce_scatter x1, waiting for transfers between devices, per_device(): lax.psum_scatter(jnp.dot(hidden_all, local_down, preferred_element_type=j...  187 us
    all_gather x1, waiting for transfers between devices, per_device(): lax.all_gather(dense_down, 'ep', axis=0, tiled=True)  170 us
    all_gather x1, waiting for transfers between devices, per_device(): piece = lax.all_gather(arrived, 'ep', axis=0, tiled=True)  166 us
    all_gather x1, waiting for transfers between devices, per_device(): up_vals = add_single(lax.all_gather(dense_up, 'ep', axis=0, tiled=True))  165 us
    all_gather x1, waiting for transfers between devices, per_device(): gate_vals = add_single(lax.all_gather(dense_gate, 'ep', axis=0, tiled=True))  99.5 us
    all_gather x1, blocking collectives, per_device(): gathered = lax.all_gather(tokens, 'tp', axis=0, tiled=True)  30.4 us
    all_to_all x1, starting transfers between devices, per_device(): lax.all_to_all(computed, 'tp', split_axis=0, concat_axis=0, tiled=True)  23.8 us
    dot_general x1, matrix products, per_device(): jnp.dot(hidden_all, local_down, preferred_element_type=jnp.float32)  22.9 us
  transfers between devices with their start and end apart: 7, of which 7 were waited for; matrix products, arithmetic and copies ran while one was open for 5% of the time, Pallas kernels for 0%

commit v1 on v0

--- a/solution.py
+++ b/solution.py
@@ -34,7 +34,11 @@
         return add_piece(gathered, weight_piece)
 
     gate_vals = add_single(lax.all_gather(dense_gate, "ep", axis=0, tiled=True))
-    up_vals = add_single(lax.all_gather(dense_up, "ep", axis=0, tiled=True))
+    up_vals = add_single(
+        jnp.concatenate(
+            lax.all_to_all(jnp.stack([dense_up] * lax.axis_size("ep")), "ep", 0, 0), axis=0
+        )
+    )
     dense_hidden = (jax.nn.silu(gate_vals) * up_vals).astype(jnp.bfloat16)
     partial_value = by_rows(dense_hidden, lax.all_gather(dense_down, "ep", axis=0, tiled=True))
     dense_out = lax.psum_scatter(

time: 954 us -> 882 us (0.925)
  waiting for transfers between devices: 814 us -> 640 us
  blocking collectives: 45.2 us -> 137 us
    all_gather x1 -> x0, waiting for transfers between devices: 165 us -> none  [per_device(): up_vals = add_single(lax.all_gather(dense_up, 'ep', axis=0, tiled=True))]
    all_gather x1, blocking collectives: 30.4 us -> 122 us  [per_device(): gathered = lax.all_gather(tokens, 'tp', axis=0, tiled=True)]
  transfers between devices with their start and end apart: 7 -> 7, of which waited for: 7 -> 6; matrix products, arithmetic and copies ran while one was open for 5% -> 6% of each run, Pallas kernels for 0% -> 0%
where the time goes in v1:
time: 882 us
  waiting for transfers between devices  640 us (73%)
  blocking collectives  137 us (16%)
  matrix products  51.4 us (6%)
  starting transfers between devices  30 us (3%)
  between operations  13.3 us (2%)
    reduce_scatter x1, waiting for transfers between devices, per_device(): lax.psum_scatter(jnp.dot(hidden_all, local_down, preferred_element_type=j...  187 us
    all_gather x1, waiting for transfers between devices, per_device(): piece = lax.all_gather(arrived, 'ep', axis=0, tiled=True)  167 us
    all_gather x1, waiting for transfers between devices, per_device(): lax.all_gather(dense_down, 'ep', axis=0, tiled=True)  164 us
    all_gather x1, blocking collectives, per_device(): gathered = lax.all_gather(tokens, 'tp', axis=0, tiled=True)  122 us
    all_gather x1, waiting for transfers between devices, per_device(): gate_vals = add_single(lax.all_gather(dense_gate, 'ep', axis=0, tiled=True))  99.9 us
    all_to_all x1, starting transfers between devices, per_device(): lax.all_to_all(computed, 'tp', split_axis=0, concat_axis=0, tiled=True)  24.1 us
    dot_general x1, matrix products, per_device(): jnp.dot(hidden_all, local_down, preferred_element_type=jnp.float32)  22.9 us
    dot_general x2, matrix products, by_rows(): lax.dot_general(left, right, (((1,), (1,)), ((), ())), preferred_element_...  22.1 us
  transfers between devices with their start and end apart: 7, of which 6 were waited for; matrix products, arithmetic and copies ran while one was open for 6% of the time, Pallas kernels for 0%

profile of v1, /device:TPU:1, one launch (start us, length us, event | category | flops | bytes accessed | tf_op | source)
XLA Modules:
  0.0 882.0 jit_solution(4012197886533688766)
XLA Ops:
  6.5 0.0 copy-start
  6.5 0.0 all-gather.8.cloned.1.call-start
  6.5 0.9 copy.14
  7.4 0.1 eq.28
  7.5 0.1 fusion.27
  7.6 0.2 select_reduce_fusion
  7.8 0.1 sub.6
  7.9 0.1 copy.16
  8.0 0.1 fusion.28
  8.1 1.2 fusion
  9.3 14.8 %all_to_all.15 = bf16[4,8,7168]{2,1,0:T(8,128)(2,1)} all-to-all(bf16[4,8,7168]{2,1,0:T(8,128)(2,1)S(1)} %fusion), channel_id=1, replica_groups=mesh['tp'=4,'ep'=32] {'tp'}, dimensions={0} | all-to-all | bytes 917504 | tf_op jit(solution)/shard_map/all_to_all | solution.py:55
  24.1 0.0 all-gather.8.cloned.1.call-update
  24.1 0.0 all-gather.4.cloned.1.call-start
  24.2 0.7 all-gather.4.cloned.1.call-update
  24.9 0.0 all-gather.6.cloned.1.call-start
  24.9 0.7 all-gather.6.cloned.1.call-update
  25.6 0.0 reduce-scatter.5.cloned.1.call-start
  25.6 166.9 %all-gather.8.cloned.1.call-done = bf16[1024,7168]{1,0:T(8,128)(2,1)} async-done(((bf16[32,7168]{1,0:T(8,128)(2,1)}), bf16[1024,7168]{1,0:T(8,128)(2,1)}) %all-gather.8.cloned.1.call-update) | async-done | bytes 14680080 | tf_op jit(solution)/shard_map/all_gather | solution.py:60
  192.5 10.8 %fusion.4 = f32[1024,152]{0,1:T(8,128)S(1)} fusion(bf16[1024,7168]{1,0:T(8,128)(2,1)} %all-gather.8.cloned.1.call-done, bf16[1,152,7168]{2,1,0:T(8,128)(2,1)} %param.17), kind=kOutput, calls=%fused_computation.9 | convolution fusion | flops 2231369728 | bytes 17481728 | tf_op jit(solution)/shard_map/dot_general | solution.py:12
  203.3 0.0 copy-done
  203.3 22.9 %convolution_convert_fusion = bf16[1024,7168]{1,0:T(8,128)(2,1)} fusion(bf16[1,152,7168]{2,1,0:T(8,128)(2,1)S(1)} %copy-done, bf16[1024,7168]{1,0:T(8,128)(2,1)} %all-gather.8.cloned.1.call-done, bf16[1,152,7168]{2,1,0:T(8,128)(2,1)} %param.18, f32[1024,152]{0,1:T(8,128)S(1)} %fusion.4), kind=kOutput, calls=%fused_computation.2 | convolution fusion | flops 4471013376 | bytes 34340864 | tf_op jit(solution)/shard_map/dot_general | solution.py:65
  226.3 0.0 copy-start.3
  226.3 0.0 reduce-scatter.5.cloned.1.call-update
  226.3 0.9 copy-done.3
  227.2 4.3 stack.2
  231.5 0.0 copy-start.2
  231.5 5.7 all-to-all-start
  237.2 0.0 reduce-scatter.3.cloned.1.call-start
  237.3 0.0 copy-done.2
  237.3 122.3 %all_gather.12 = bf16[32,7168]{1,0:T(8,128)(2,1)S(1)} all-gather(bf16[8,7168]{1,0:T(8,128)(2,1)S(1)} %copy-done.2), channel_id=1, replica_groups=mesh['tp'=4,'ep'=32] {'tp'}, dimensions={0}, use_global_device_ids=true | all-gather | bytes 573440 | tf_op jit(solution)/shard_map/all_gather | solution.py:31
  359.5 99.9 %all-gather.4.cloned.1.call-done = bf16[7168,640]{1,0:T(8,128)(2,1)} async-done(((bf16[224,640]{1,0:T(8,128)(2,1)}), bf16[7168,640]{1,0:T(8,128)(2,1)}) %all-gather.4.cloned.1.call-update) | async-done | bytes 9175056 | tf_op jit(solution)/shard_map/all_gather | solution.py:36
  459.4 5.1 fusion.31
  464.5 0.0 all-to-all-done
  464.5 163.6 %all-gather.6.cloned.1.call-done = bf16[7168,640]{1,0:T(8,128)(2,1)} async-done(((bf16[224,640]{1,0:T(8,128)(2,1)}), bf16[7168,640]{1,0:T(8,128)(2,1)}) %all-gather.6.cloned.1.call-update) | async-done | bytes 9175056 | tf_op jit(solution)/shard_map/all_gather | solution.py:43
  628.1 0.0 copy-start.1
  628.1 0.0 copy-start.4
  628.1 11.4 %convolution_convert_fusion.2 = bf16[32,7168]{1,0:T(8,128)(2,1)} fusion(bf16[7168,640]{1,0:T(8,128)(2,1)} %all-gather.6.cloned.1.call-done, bf16[32,7168]{1,0:T(8,128)(2,1)S(1)} %all_gather.12, bf16[7168,640]{1,0:T(8,128)(2,1)} %bitcast, f32[32,640]{1,0:T(8,128)S(1)} %fusion.31), kind=kOutput, calls=%fused_computation.4 | convolution fusion | flops 587554816 | bytes 19349504 | tf_op jit(solution)/shard_map/dot_general | solution.py:12
  639.4 0.0 reduce-scatter.3.cloned.1.call-update
  639.5 0.2 slice_reduce_fusion.1
  639.7 186.7 %reduce-scatter.5.cloned.1.call-done = bf16[32,7168]{1,0:T(8,128)(2,1)} async-done(((bf16[1024,7168]{1,0:T(8,128)(2,1)}), bf16[32,7168]{1,0:T(8,128)(2,1)}) %reduce-scatter.5.cloned.1.call-update) | async-done | bytes 458768 | tf_op jit(solution)/shard_map/reduce_scatter | solution.py:64
  826.3 24.1 %all-to-all-start.2 = ((bf16[4,8,7168]{2,1,0:T(8,128)(2,1)}), bf16[4,8,7168]{2,1,0:T(8,128)(2,1)S(1)}, u32[]{:S(2)}, u32[]{:S(2)}) async-start(bf16[4,8,7168]{2,1,0:T(8,128)(2,1)} %bitcast.37), calls=%async_computation.4 | async-start | bytes 917504 | tf_op jit(solution)/shard_map/all_to_all | solution.py:71
  850.5 0.0 copy-done.4
  850.5 8.7 all-to-all-done.2
  859.2 0.6 gather_fusion
  859.9 0.6 gather_fusion.1
  860.5 13.3 %reduce-scatter.3.cloned.1.call-done = bf16[8,7168]{1,0:T(8,128)(2,1)} async-done(((bf16[32,7168]{1,0:T(8,128)(2,1)}), bf16[8,7168]{1,0:T(8,128)(2,1)}) %reduce-scatter.3.cloned.1.call-update) | async-done | bytes 114704 | tf_op jit(solution)/shard_map/reduce_scatter | solution.py:44
  873.8 1.7 add_convert_fusion
  875.5 0.0 copy-done.1
  (8 shorter events, 0.1 us)
Async XLA Ops:
  6.5 196.8 %copy-start = (bf16[1,152,7168]{2,1,0:T(8,128)(2,1)S(1)}, bf16[1,152,7168]{2,1,0:T(8,128)(2,1)}, u32[]{:S(2)}) copy-start(bf16[1,152,7168]{2,1,0:T(8,128)(2,1)} %param.19) | copy-start | bytes 6537220
  6.5 186.0 %all-gather.8.cloned.1.call-start = ((), (), s32[]{:S(2)}) async-start(), calls=%async_computation.8 | async-start | bytes 15138816 | tf_op jit(solution)/shard_map/all_gather | solution.py:60
  24.1 435.3 %all-gather.4.cloned.1.call-start = ((), (), s32[]{:S(2)}) async-start(), calls=%async_computation.5 | async-start | bytes 9461760 | tf_op jit(solution)/shard_map/all_gather | solution.py:36
  24.9 603.2 %all-gather.6.cloned.1.call-start = ((), (), s32[]{:S(2)}) async-start(), calls=%async_computation.6 | async-start | bytes 9461760 | tf_op jit(solution)/shard_map/all_gather | solution.py:43
  25.6 800.7 %reduce-scatter.5.cloned.1.call-start = ((), (), s32[]{:S(2)}) async-start(), calls=%async_computation.9 | async-start | bytes 15138816 | tf_op jit(solution)/shard_map/reduce_scatter | solution.py:64
  226.3 1.0 copy-start.3
  231.5 5.8 copy-start.2
  231.5 233.0 %all-to-all-start = ((bf16[32,224,640]{2,1,0:T(8,128)(2,1)}), bf16[32,224,640]{2,1,0:T(8,128)(2,1)}, u32[]{:S(2)}, u32[]{:S(2)}) async-start(bf16[32,224,640]{2,1,0:T(8,128)(2,1)} %stack.2), calls=%async_computation | async-start | bytes 18350080 | tf_op jit(solution)/shard_map/all_to_all | solution.py:39
  237.2 636.6 %reduce-scatter.3.cloned.1.call-start = ((), (), s32[]{:S(2)}) async-start(), calls=%async_computation.7 | async-start | bytes 573440 | tf_op jit(solution)/shard_map/reduce_scatter | solution.py:44
  628.1 247.4 %copy-start.1 = (bf16[1,152,7168]{2,1,0:T(8,128)(2,1)S(1)}, bf16[1,152,7168]{2,1,0:T(8,128)(2,1)}, u32[]{:S(2)}) copy-start(bf16[1,152,7168]{2,1,0:T(8,128)(2,1)} %param.19) | copy-start | bytes 6537220
  628.1 222.4 %copy-start.4 = (f32[8,2]{0,1:T(2,128)S(1)}, f32[8,2]{0,1:T(2,128)}, u32[]{:S(2)}) copy-start(f32[8,2]{0,1:T(2,128)} %param.13) | copy-start | bytes 196
  826.3 32.9 %all-to-all-start.2 = ((bf16[4,8,7168]{2,1,0:T(8,128)(2,1)}), bf16[4,8,7168]{2,1,0:T(8,128)(2,1)S(1)}, u32[]{:S(2)}, u32[]{:S(2)}) async-start(bf16[4,8,7168]{2,1,0:T(8,128)(2,1)} %bitcast.37), calls=%async_computation.4 | async-start | bytes 917504 | tf_op jit(solution)/shard_map/all_to_all | solution.py:71
Sparse Core Ops, SparseCore 0:
  24.2 168.2 all-gather.7
  194.2 265.1 all-gather.3
  461.1 166.9 all-gather.5
  630.4 195.9 reduce-scatter.4
  828.8 44.9 reduce-scatter.2
